TPU v7x, 256 devices: a whole 4x4x8 slice. The times are simulated.
256 devices in a mesh: clip: 8 (over z), blk: 8 (over y_hi, x), head: 4 (over y_lo, core).
Axes of the slice: x: 4, y: 4 (y_hi: 2, y_lo: 2; y = y_hi * 2 + y_lo), z: 8, core: 2. Of those that a mesh axis runs over, the one named last changes fastest.
Arguments:
- q_in: bfloat16 [32768, 2560], P(('clip', 'blk', 'head')), parts along dimension 0, may hold values from -4 to 4
- k_in: bfloat16 [32768, 2560], P(('clip', 'blk', 'head')), parts along dimension 0, may hold values from -4 to 4
- v_in: bfloat16 [32768, 2560], P(('clip', 'blk', 'head')), parts along dimension 0, may hold values from -6 to 6
- q_gain: float32 [2560], replicated, may hold values from 0.5 to 2
- k_gain: float32 [2560], replicated, may hold values from 0.5 to 2
- out_weight: bfloat16 [2560, 5120], P('head'), may hold values from -0.125 to 0.125
- out_bias: float32 [5120], replicated, may hold values from -3 to 3
- out_gate: float32 [5120], replicated, may hold values from -4 to 4
Outputs:
- branch_out: bfloat16 [32768, 5120], P(('clip', 'blk', 'head')), parts along dimension 0
There are 8 independent parts, one for each index of `clip`. A program takes and returns all parts, laid end to end along the dimension named above; an argument that names none is the same for every part. Nothing has to cross between parts.
All inputs are finite; a program needn't handle non-finite values.
Results may differ from a plain program's by a relative error of at most 0.008.
Values may be sent and summed in bfloat16 or wider, within the bound.
A program may use at most 128 MiB of HBM per device.

v0:
```python
import jax
import jax.numpy as jnp
from jax import lax
from jax.sharding import PartitionSpec as P

HD = 128


def normalize(values, gain):
    wide = values.astype(jnp.float32)
    factor = lax.rsqrt(jnp.mean(wide * wide, axis=-1, keepdims=True) + 1e-06)
    return (wide * factor * gain).astype(jnp.bfloat16)


def body(q_in, k_in, v_in, q_gain, k_gain, out_weight, out_bias, out_gate):
    queries = normalize(q_in, q_gain)
    keys = normalize(k_in, k_gain)
    head_q, head_k, head_v = (
        lax.all_to_all(queries, "head", split_axis=1, concat_axis=0, tiled=True),
        lax.all_to_all(keys, "head", split_axis=1, concat_axis=0, tiled=True),
        lax.all_to_all(v_in, "head", split_axis=1, concat_axis=0, tiled=True),
    )
    row_count = head_q.shape[0]
    head_count = head_q.shape[1] // HD
    query_blocks = head_q.reshape(row_count, head_count, HD)

    def block_step(state_now, block_pair):
        key_block, value_block = block_pair
        scores = jnp.einsum(
            "rhd,khd->hrk", query_blocks, key_block, preferred_element_type=jnp.float32
        ) * HD ** (-0.5)
        running, summed, mixed = state_now
        highest = jnp.maximum(running, jnp.max(scores, axis=-1))
        shrink = jnp.exp(running - highest)
        weights = jnp.exp(scores - highest[:, :, None])
        summed = summed * shrink + jnp.sum(weights, axis=-1)
        added = jnp.einsum(
            "hrk,khd->rhd",
            weights.astype(jnp.bfloat16),
            value_block,
            preferred_element_type=jnp.float32,
        )
        mixed = mixed * shrink.T[:, :, None] + added
        return ((highest, summed, mixed), None)

    start_state = (
        jnp.full((head_count, row_count), -jnp.inf, jnp.float32),
        jnp.zeros((head_count, row_count), jnp.float32),
        jnp.zeros((row_count, head_count, HD), jnp.float32),
    )
    state_now = start_state
    key_piece = lax.all_gather(head_k, "blk", axis=0, tiled=True)
    value_piece = lax.all_gather(head_v, "blk", axis=0, tiled=True)
    length = key_piece.shape[0]
    key_three = key_piece.reshape(length, head_count, HD)
    value_three = value_piece.reshape(length, head_count, HD)
    key_stack = key_three.reshape(length // 1024, 1024, head_count, HD)
    value_stack = value_three.reshape(length // 1024, 1024, head_count, HD)
    state_now, unused = lax.scan(block_step, state_now, (key_stack, value_stack))
    highest, summed, mixed = state_now
    attended = (
        (mixed / summed.T[:, :, None]).astype(jnp.bfloat16).reshape(row_count, head_count * HD)
    )
    projected = lax.psum_scatter(
        jnp.dot(attended, out_weight, preferred_element_type=jnp.float32).astype(jnp.bfloat16),
        "head",
        scatter_dimension=0,
        tiled=True,
    ).astype(jnp.float32)
    return (out_gate * (projected + out_bias)).astype(jnp.bfloat16)


def solution(mesh):
    in_specs = (
        P(("clip", "blk", "head"), None),
        P(("clip", "blk", "head"), None),
        P(("clip", "blk", "head"), None),
        P(),
        P(),
        P("head", None),
        P(),
        P(),
    )
    out_specs = P(("clip", "blk", "head"), None)
    return jax.shard_map(body, mesh=mesh, in_specs=in_specs, out_specs=out_specs, check_vma=False)
```

profile of v0, /device:TPU:1, one launch (start us, length us, event | category | flops | bytes accessed | tf_op | source)
XLA Modules:
  0.0 359.6 jit_solution(15546588025811815975)
XLA Ops:
  6.5 1.4 copy.29
  8.0 0.4 fusion.23
  8.3 1.1 fusion.25
  9.4 14.9 %all_to_all.54 = bf16[128,4,640]{0,2,1:T(8,128)(2,1)S(1)} all-to-all(bf16[128,4,640]{0,2,1:T(8,128)(2,1)S(1)} %bitcast.62), channel_id=1, replica_groups=mesh['clip'=8,'blk'=8,'head'=4] {'head'}, dimensions={1} | all-to-all | bytes 1310720 | tf_op jit(solution)/shard_map/all_to_all | solution.py:20
  24.3 1.1 copy.30
  25.4 0.0 all-gather.3.cloned.1.call-update
  25.4 0.0 copy-start.5
  25.4 0.0 all-gather.5.cloned.1.call-start
  25.5 0.3 copy.34
  25.8 12.7 %all_to_all.55 = bf16[128,4,640]{0,2,1:T(8,128)(2,1)S(1)} all-to-all(bf16[128,4,640]{0,2,1:T(8,128)(2,1)S(1)} %bitcast.65), channel_id=1, replica_groups=mesh['clip'=8,'blk'=8,'head'=4] {'head'}, dimensions={1} | all-to-all | bytes 1310720 | tf_op jit(solution)/shard_map/all_to_all | solution.py:21
  38.5 1.1 copy.35
  39.6 0.0 all-gather.5.cloned.1.call-update
  39.6 0.2 fusion.26
  39.8 0.2 fusion.28
  40.1 1.1 copy.32
  41.1 4.5 %all-to-all-start.1 = ((bf16[128,4,640]{0,2,1:T(8,128)(2,1)}), bf16[128,4,640]{0,2,1:T(8,128)(2,1)S(1)}, u32[]{:S(2)}, u32[]{:S(2)}) async-start(bf16[128,4,640]{0,2,1:T(8,128)(2,1)} %bitcast.3), calls=%async_computation.1 | async-start | bytes 1310720 | tf_op jit(solution)/shard_map/all_to_all | solution.py:19
  45.6 11.5 %all-to-all-done.1 = bf16[128,4,640]{0,2,1:T(8,128)(2,1)S(1)} async-done(((bf16[128,4,640]{0,2,1:T(8,128)(2,1)}), bf16[128,4,640]{0,2,1:T(8,128)(2,1)S(1)}, u32[]{:S(2)}, u32[]{:S(2)}) %all-to-all-start.1) | async-done | bytes 655392 | tf_op jit(solution)/shard_map/all_to_all | solution.py:19
  57.1 0.5 copy.33
  57.6 0.2 reshape.39
  57.9 0.3 copy.38
  58.2 55.0 %all-gather.3.cloned.1.call-done = bf16[4096,640]{1,0:T(8,128)(2,1)} async-done(((bf16[512,640]{1,0:T(8,128)(2,1)}), bf16[4096,640]{1,0:T(8,128)(2,1)}) %all-gather.3.cloned.1.call-update) | async-done | bytes 5242896 | tf_op jit(solution)/shard_map/all_gather | solution.py:52
  113.2 12.6 %reshape.41 = bf16[4,1024,5,128]{3,2,1,0:T(8,128)(2,1)} reshape(bf16[4096,640]{1,0:T(8,128)(2,1)} %all-gather.3.cloned.1.call-done) | data formatting | bytes 10485760 | tf_op jit(solution)/shard_map/reshape;reshape | solution.py:57
  125.8 7.5 %copy.37 = bf16[4,1024,5,128]{3,1,2,0:T(8,128)(2,1)} copy(bf16[4,1024,5,128]{3,2,1,0:T(8,128)(2,1)} %reshape.41) | data formatting | bytes 10485760
  133.3 65.9 %all-gather.5.cloned.1.call-done = bf16[4096,640]{1,0:T(8,128)(2,1)} async-done(((bf16[512,640]{1,0:T(8,128)(2,1)}), bf16[4096,640]{1,0:T(8,128)(2,1)}) %all-gather.5.cloned.1.call-update) | async-done | bytes 5242896 | tf_op jit(solution)/shard_map/all_gather | solution.py:53
  199.2 12.6 %reshape.42 = bf16[4,1024,5,128]{3,2,1,0:T(8,128)(2,1)} reshape(bf16[4096,640]{1,0:T(8,128)(2,1)} %all-gather.5.cloned.1.call-done) | data formatting | bytes 10485760 | tf_op jit(solution)/shard_map/reshape;reshape | solution.py:58
  211.8 11.1 %copy.39 = bf16[4,1024,5,128]{1,3,2,0:T(8,128)(2,1)} copy(bf16[4,1024,5,128]{3,2,1,0:T(8,128)(2,1)} %reshape.42) | data formatting | bytes 10485760
  222.8 63.2 %while.15 = (s32[]{:T(128)}, f32[5,512]{1,0:T(8,128)S(1)}, f32[5,512]{1,0:T(8,128)S(1)}, f32[512,5,128]{0,2,1:T(8,128)S(1)}, bf16[4,1024,5,128]{3,1,2,0:T(8,128)...) while((s32[]{:T(128)}, f32[5,512]{1,0:T(8,128)S(1)}, ...), condition=%wide.region_5.6_spmd.clone, body=%wide.region_2.5_spmd.clone.sunk | while | flops 1364147200 | bytes 79463552 | solution.py:59
  222.8 6.7 %bitcast_reduce_fusion.2 = (f32[5,512]{1,0:T(8,128)S(1)}, f32[5,1024,512]{2,1,0:T(8,128)}) fusion(bf16[512,5,128]{2,0,1:T(8,128)(2,1)S(1)} %get-tuple-element.182, bf16[4,1024,5,128]{3,1,2,0:T(8,128)(2,1)} %get-tuple-element.181, s32[]{:T(128)} %get-tuple-element.168), kind=kOutput, calls=%fused_computation.1.clone.1 | convolution fusion | flops 676328960 | bytes 12462592 | tf_op jit(solution)/shard_map/while/body/eval_jaxpr/rhd,khd->hrk/dot_general | solution.py:29
  229.5 6.7 %fusion.45 = f32[512,5,128]{0,2,1:T(8,128)S(1)} fusion(f32[5,1024,512]{2,1,0:T(8,128)} %get-tuple-element.157, f32[5,512]{1,0:T(8,128)S(1)} %get-tuple-element.178, f32[512,5,128]{0,2,1:T(8,128)S(1)} %get-tuple-element.171, bf16[4,1024,5,128]{1,3,2,0:T(8,128)(2,1)} %get-tuple-element.183, s32[]{:T(128)} %get-tuple-element.168, ...), kind=kOutput, calls=%fused_computation.9.clone.1 | convolution fusion | flops 679936000 | bytes 14438913 | tf_op jit(solution)/shard_map/while/body/eval_jaxpr/hrk,khd->rhd/dot_general | solution.py:37
  236.2 0.7 copy-done
  236.9 1.7 fusion.43
  238.6 6.7 %bitcast_reduce_fusion.2 = (f32[5,512]{1,0:T(8,128)S(1)}, f32[5,1024,512]{2,1,0:T(8,128)}) fusion(bf16[512,5,128]{2,0,1:T(8,128)(2,1)S(1)} %get-tuple-element.182, bf16[4,1024,5,128]{3,1,2,0:T(8,128)(2,1)} %get-tuple-element.181, s32[]{:T(128)} %get-tuple-element.168), kind=kOutput, calls=%fused_computation.1.clone.1 | convolution fusion | flops 676328960 | bytes 12462592 | tf_op jit(solution)/shard_map/while/body/eval_jaxpr/rhd,khd->hrk/dot_general | solution.py:29
  245.3 6.7 %fusion.45 = f32[512,5,128]{0,2,1:T(8,128)S(1)} fusion(f32[5,1024,512]{2,1,0:T(8,128)} %get-tuple-element.157, f32[5,512]{1,0:T(8,128)S(1)} %get-tuple-element.178, f32[512,5,128]{0,2,1:T(8,128)S(1)} %get-tuple-element.171, bf16[4,1024,5,128]{1,3,2,0:T(8,128)(2,1)} %get-tuple-element.183, s32[]{:T(128)} %get-tuple-element.168, ...), kind=kOutput, calls=%fused_computation.9.clone.1 | convolution fusion | flops 679936000 | bytes 14438913 | tf_op jit(solution)/shard_map/while/body/eval_jaxpr/hrk,khd->rhd/dot_general | solution.py:37
  252.0 0.7 copy-done
  252.7 1.7 fusion.43
  254.4 6.7 %bitcast_reduce_fusion.2 = (f32[5,512]{1,0:T(8,128)S(1)}, f32[5,1024,512]{2,1,0:T(8,128)}) fusion(bf16[512,5,128]{2,0,1:T(8,128)(2,1)S(1)} %get-tuple-element.182, bf16[4,1024,5,128]{3,1,2,0:T(8,128)(2,1)} %get-tuple-element.181, s32[]{:T(128)} %get-tuple-element.168), kind=kOutput, calls=%fused_computation.1.clone.1 | convolution fusion | flops 676328960 | bytes 12462592 | tf_op jit(solution)/shard_map/while/body/eval_jaxpr/rhd,khd->hrk/dot_general | solution.py:29
  261.1 6.7 %fusion.45 = f32[512,5,128]{0,2,1:T(8,128)S(1)} fusion(f32[5,1024,512]{2,1,0:T(8,128)} %get-tuple-element.157, f32[5,512]{1,0:T(8,128)S(1)} %get-tuple-element.178, f32[512,5,128]{0,2,1:T(8,128)S(1)} %get-tuple-element.171, bf16[4,1024,5,128]{1,3,2,0:T(8,128)(2,1)} %get-tuple-element.183, s32[]{:T(128)} %get-tuple-element.168, ...), kind=kOutput, calls=%fused_computation.9.clone.1 | convolution fusion | flops 679936000 | bytes 14438913 | tf_op jit(solution)/shard_map/while/body/eval_jaxpr/hrk,khd->rhd/dot_general | solution.py:37
  267.8 0.7 copy-done
  268.5 1.7 fusion.43
  270.2 6.7 %bitcast_reduce_fusion.2 = (f32[5,512]{1,0:T(8,128)S(1)}, f32[5,1024,512]{2,1,0:T(8,128)}) fusion(bf16[512,5,128]{2,0,1:T(8,128)(2,1)S(1)} %get-tuple-element.182, bf16[4,1024,5,128]{3,1,2,0:T(8,128)(2,1)} %get-tuple-element.181, s32[]{:T(128)} %get-tuple-element.168), kind=kOutput, calls=%fused_computation.1.clone.1 | convolution fusion | flops 676328960 | bytes 12462592 | tf_op jit(solution)/shard_map/while/body/eval_jaxpr/rhd,khd->hrk/dot_general | solution.py:29
  276.9 6.7 %fusion.45 = f32[512,5,128]{0,2,1:T(8,128)S(1)} fusion(f32[5,1024,512]{2,1,0:T(8,128)} %get-tuple-element.157, f32[5,512]{1,0:T(8,128)S(1)} %get-tuple-element.178, f32[512,5,128]{0,2,1:T(8,128)S(1)} %get-tuple-element.171, bf16[4,1024,5,128]{1,3,2,0:T(8,128)(2,1)} %get-tuple-element.183, s32[]{:T(128)} %get-tuple-element.168, ...), kind=kOutput, calls=%fused_computation.9.clone.1 | convolution fusion | flops 679936000 | bytes 14438913 | tf_op jit(solution)/shard_map/while/body/eval_jaxpr/hrk,khd->rhd/dot_general | solution.py:37
  283.6 0.7 copy-done
  284.2 1.7 fusion.43
  286.0 0.2 divide_convert_fusion
  286.2 8.9 %convolution_convert_fusion = bf16[512,5120]{1,0:T(8,128)(2,1)} fusion(bf16[512,640]{0,1:T(8,128)(2,1)S(1)} %bitcast.66, bf16[640,5120]{1,0:T(8,128)(2,1)} %param.15), kind=kOutput, calls=%fused_computation.24 | convolution fusion | flops 3358064640 | bytes 12451840 | tf_op jit(solution)/shard_map/dot_general | solution.py:65
  295.1 0.0 reduce-scatter.2.cloned.1.call-update
  295.1 55.3 %reduce-scatter.2.cloned.1.call-done = bf16[128,5120]{1,0:T(8,128)(2,1)} async-done(((bf16[512,5120]{1,0:T(8,128)(2,1)}), bf16[128,5120]{1,0:T(8,128)(2,1)}) %reduce-scatter.2.cloned.1.call-update) | async-done | bytes 1310736 | tf_op jit(solution)/shard_map/reduce_scatter | solution.py:64
  350.4 2.7 multiply_convert_fusion
  (32 shorter events, 0.2 us)
Async XLA Ops:
  6.5 106.6 %all-gather.3.cloned.1.call-start = ((), (), s32[]{:S(2)}) async-start(), calls=%async_computation.4 | async-start | bytes 5898240 | tf_op jit(solution)/shard_map/all_gather | solution.py:52
  7.9 17.5 %copy-start.2 = (bf16[128,2560]{1,0:T(8,128)(2,1)S(1)}, bf16[128,2560]{1,0:T(8,128)(2,1)}, u32[]{:S(2)}) copy-start(bf16[128,2560]{1,0:T(8,128)(2,1)} %param.12) | copy-start | bytes 1966084
  25.4 14.2 %copy-start.1 = (bf16[128,2560]{1,0:T(8,128)(2,1)S(1)}, bf16[128,2560]{1,0:T(8,128)(2,1)}, u32[]{:S(2)}) copy-start(bf16[128,2560]{1,0:T(8,128)(2,1)} %param.10) | copy-start | bytes 1966084
  25.4 14.4 %copy-start.5 = (f32[2560]{0:T(1024)S(1)}, f32[2560]{0:T(1024)}, u32[]{:S(2)}) copy-start(f32[2560]{0:T(1024)} %param.13) | copy-start | bytes 30724
  25.4 173.7 %all-gather.5.cloned.1.call-start = ((), (), s32[]{:S(2)}) async-start(), calls=%async_computation.5 | async-start | bytes 5898240 | tf_op jit(solution)/shard_map/all_gather | solution.py:53
  41.1 16.0 %all-to-all-start.1 = ((bf16[128,4,640]{0,2,1:T(8,128)(2,1)}), bf16[128,4,640]{0,2,1:T(8,128)(2,1)S(1)}, u32[]{:S(2)}, u32[]{:S(2)}) async-start(bf16[128,4,640]{0,2,1:T(8,128)(2,1)} %bitcast.3), calls=%async_computation.1 | async-start | bytes 1310720 | tf_op jit(solution)/shard_map/all_to_all | solution.py:19
  45.6 304.7 %reduce-scatter.2.cloned.1.call-start = ((), (), s32[]{:S(2)}) async-start(), calls=%async_computation.6 | async-start | bytes 6553600 | tf_op jit(solution)/shard_map/reduce_scatter | solution.py:64
  229.5 7.4 %copy-start = (f32[5,1024,512]{2,1,0:T(8,128)S(1)}, f32[5,1024,512]{2,1,0:T(8,128)}, u32[]{:S(2)}) copy-start(f32[5,1024,512]{2,1,0:T(8,128)} %get-tuple-element.157) | copy-start | bytes 31457284 | tf_op jit(solution)/shard_map/while
  245.3 7.4 %copy-start = (f32[5,1024,512]{2,1,0:T(8,128)S(1)}, f32[5,1024,512]{2,1,0:T(8,128)}, u32[]{:S(2)}) copy-start(f32[5,1024,512]{2,1,0:T(8,128)} %get-tuple-element.157) | copy-start | bytes 31457284 | tf_op jit(solution)/shard_map/while
  261.1 7.4 %copy-start = (f32[5,1024,512]{2,1,0:T(8,128)S(1)}, f32[5,1024,512]{2,1,0:T(8,128)}, u32[]{:S(2)}) copy-start(f32[5,1024,512]{2,1,0:T(8,128)} %get-tuple-element.157) | copy-start | bytes 31457284 | tf_op jit(solution)/shard_map/while
  276.9 7.4 %copy-start = (f32[5,1024,512]{2,1,0:T(8,128)S(1)}, f32[5,1024,512]{2,1,0:T(8,128)}, u32[]{:S(2)}) copy-start(f32[5,1024,512]{2,1,0:T(8,128)} %get-tuple-element.157) | copy-start | bytes 31457284 | tf_op jit(solution)/shard_map/while
  295.1 55.3 %copy-start.3 = (f32[5120]{0:T(1024)S(1)}, f32[5120]{0:T(1024)}, u32[]{:S(2)}) copy-start(f32[5120]{0:T(1024)} %param.16) | copy-start | bytes 61444
  295.1 55.3 %copy-start.4 = (f32[5120]{0:T(1024)S(1)}, f32[5120]{0:T(1024)}, u32[]{:S(2)}) copy-start(f32[5120]{0:T(1024)} %param.17) | copy-start | bytes 61444
Sparse Core Ops, SparseCore 0:
  25.5 87.6 all-gather.2
  115.8 83.3 all-gather.4
  295.2 55.1 reduce-scatter.1
where the time goes:
time: 361 us; the launch traced here: 360 us
  waiting for transfers between devices  188 us (52%)
  matrix products  62.2 us (17%)
  local copies, waits for them, and re-layouts  52.6 us (15%)
  blocking collectives  27.5 us (8%)
  between operations  13.2 us (4%)
  other arithmetic  11.7 us (3%)
  starting transfers between devices  4.53 us (1%)
    all_gather x1, waiting for transfers between devices, body(): value_piece = lax.all_gather(head_v, 'blk', axis=0, tiled=True)  65.9 us
    reduce_scatter x1, waiting for transfers between devices, body(): lax.psum_scatter(jnp.dot(attended, out_weight, preferred_element_type=jnp...  55.3 us
    all_gather x1, waiting for transfers between devices, body(): key_piece = lax.all_gather(head_k, 'blk', axis=0, tiled=True)  55 us
    dot_general x4, matrix products, block_step(): jnp.einsum('hrk,khd->rhd', weights.astype(jnp.bfloat16), value_block, pre...  26.7 us
    dot_general x4, matrix products, block_step(): jnp.einsum('rhd,khd->hrk', query_blocks, key_block, preferred_element_typ...  26.6 us
    unnamed x15, local copies, waits for them, and re-layouts  20.6 us
    all_to_all x1, blocking collectives, body(): lax.all_to_all(keys, 'head', split_axis=1, concat_axis=0, tiled=True)  14.9 us
    all_to_all x1, blocking collectives, body(): lax.all_to_all(v_in, 'head', split_axis=1, concat_axis=0, tiled=True)  12.7 us
  transfers between devices with their start and end apart: 4, of which 4 were waited for; matrix products, arithmetic and copies ran while one was open for 7% of the time, Pallas kernels for 0%

commit v1 on v0

v1 whole, which is shorter than its diff:
```python
import functools
import math

import jax
import jax.numpy as jnp
from jax import lax
from jax.experimental import pallas as pl
from jax.experimental.pallas import tpu as pltpu
from jax.sharding import PartitionSpec as P

HD = 128
SIDE = 4
CHIPS = SIDE * SIDE
CLASS_HEADS = 10
HEADS = 20
KEY_CHUNK = 512
OUT_CHUNK = 512
MESH = pl.DeviceIdType.MESH


def kernel(
    q_ref, k_ref, v_ref, qg_ref, kg_ref, w_ref, bias_ref, gate_ref, out_ref,
    stage, qkv, scores, mixed, attended, weight, own, part_out, part_in,
    local_sem, full_send, full_recv, left_send, left_recv, row_send, row_recv,
    pair_send, pair_recv, pair_left_send, pair_left_recv, w_send, w_recv,
    mix_send, mix_recv, part_send, part_recv,
):
    tile = q_ref.shape[0]
    half = tile // 2
    keys = 2 * CHIPS * tile
    width = out_ref.shape[1]
    blk, head = lax.axis_index("blk"), lax.axis_index("head")
    x, core = lax.rem(blk, SIDE), lax.rem(head, 2)
    y = 2 * (blk // SIDE) + head // 2

    def chip(dy, dx):
        return lax.rem(y + dy, SIDE), lax.rem(x + dx, SIDE)

    def device(dy, dx):
        yy, xx = chip(dy, dx)
        return {"blk": (yy // 2) * SIDE + xx, "head": lax.rem(yy, 2) * 2 + core}

    sibling = {"blk": blk, "head": (head // 2) * 2 + 1 - core}

    def full_head(yy, xx):
        return CLASS_HEADS * lax.rem(yy, 2) + SIDE * (yy // 2) + xx

    def left_head(yy):
        return CLASS_HEADS * lax.rem(yy, 2) + 2 * SIDE + yy // 2

    def rows(start, size):
        return pl.ds(pl.multiple_of(start, half), size)

    def remote(src, dst, send, recv, target):
        return pltpu.make_async_remote_copy(
            src_ref=src, dst_ref=dst, send_sem=send, recv_sem=recv,
            device_id=target, device_id_type=MESH,
        )

    own_weight = pltpu.make_async_copy(w_ref, weight.at[core], local_sem.at[2])
    own_weight.start()

    barrier = pltpu.get_barrier_semaphore()

    def greet(r, carry):
        pl.semaphore_signal(
            barrier, inc=1, device_id=device(r // SIDE, lax.rem(r, SIDE)), device_id_type=MESH
        )
        return carry

    lax.fori_loop(1, CHIPS, greet, 0)
    pl.semaphore_signal(barrier, inc=1, device_id=sibling, device_id_type=MESH)

    def normalize(ref, gain_ref, which, scale):
        wide = ref[...].astype(jnp.float32)
        factor = lax.rsqrt(jnp.mean(wide * wide, axis=-1, keepdims=True) + 1e-06)
        for h in range(HEADS):
            cols = slice(h * HD, (h + 1) * HD)
            gain = gain_ref[:, cols] * scale if scale is not None else gain_ref[:, cols]
            stage[which, h] = (ref[:, cols].astype(jnp.float32) * factor * gain).astype(jnp.bfloat16)

    normalize(q_ref, qg_ref, 0, HD ** (-0.5) * math.log2(math.e))
    normalize(k_ref, kg_ref, 1, None)
    for h in range(HEADS):
        stage[2, h] = v_ref[:, h * HD : (h + 1) * HD]

    pl.semaphore_wait(barrier, CHIPS)

    w_copy = remote(w_ref, weight.at[core], w_send, w_recv, sibling)
    w_copy.start()

    def left_copy(dy):
        yy, xx = chip(dy, 0)
        return remote(
            stage.at[:, left_head(yy)], qkv.at[1, :, rows(dy * tile, tile), :],
            left_send.at[dy], left_recv.at[dy], device(dy, 0),
        )

    def full_copy(r):
        dy, dx = r // SIDE, lax.rem(r, SIDE)
        yy, xx = chip(dy, dx)
        return remote(
            stage.at[:, full_head(yy, xx)], qkv.at[0, :, rows(r * tile, tile), :],
            full_send.at[r], full_recv.at[r], device(dy, dx),
        )

    def pair_copy(r):
        here = qkv.at[0, pl.ds(1, 2), rows(r * tile, tile), :]
        there = qkv.at[0, pl.ds(1, 2), rows((CHIPS + r) * tile, tile), :]
        return remote(here, there, pair_send.at[r], pair_recv.at[r], sibling)

    def row_copy(dx):
        here = qkv.at[1, pl.ds(1, 2), rows(0, SIDE * tile), :]
        there = qkv.at[1, pl.ds(1, 2), rows(dx * SIDE * tile, SIDE * tile), :]
        return remote(here, there, row_send.at[dx], row_recv.at[dx], device(0, dx))

    def pair_left_copy(dx):
        here = qkv.at[1, pl.ds(1, 2), rows(dx * SIDE * tile, SIDE * tile), :]
        there = qkv.at[1, pl.ds(1, 2), rows((CHIPS + dx * SIDE) * tile, SIDE * tile), :]
        return remote(here, there, pair_left_send.at[dx], pair_left_recv.at[dx], sibling)

    def over(first, last, act):
        def step(i, carry):
            act(i)
            return carry

        lax.fori_loop(first, last, step, 0)

    over(1, SIDE, lambda dy: left_copy(dy).start())
    over(1, CHIPS, lambda r: full_copy(r).start())
    own_full = pltpu.make_async_copy(
        stage.at[:, full_head(y, x)], qkv.at[0, :, pl.ds(0, tile), :], local_sem.at[0]
    )
    own_left = pltpu.make_async_copy(
        stage.at[:, left_head(y)], qkv.at[1, :, pl.ds(0, tile), :], local_sem.at[1]
    )
    own_full.start()
    own_left.start()
    own_full.wait()
    own_left.wait()
    pair_copy(0).start()

    over(1, SIDE, lambda dy: left_copy(dy).wait_recv())
    over(1, SIDE, lambda dx: row_copy(dx).start())
    pair_left_copy(0).start()

    def pass_on(r):
        full_copy(r).wait_recv()
        pair_copy(r).start()

    over(1, CHIPS, pass_on)

    def pass_on_left(dx):
        row_copy(dx).wait_recv()
        pair_left_copy(dx).start()

    over(1, SIDE, pass_on_left)
    over(0, CHIPS, lambda r: pair_copy(r).wait_recv())
    over(0, SIDE, lambda dx: pair_left_copy(dx).wait_recv())

    def mix_copy(b):
        is_left = b // (2 * SIDE)
        t = b - 2 * SIDE * is_left
        ey = jnp.where(is_left == 1, 2 * t, 2 * (t // SIDE))
        dx = jnp.where(is_left == 1, 0, lax.rem(t, SIDE))
        slot = jnp.where(is_left == 1, 2 * SIDE + y // 2, SIDE * (y // 2) + x)
        lanes = pl.ds(pl.multiple_of(slot * HD, HD), HD)
        return remote(
            mixed.at[b], attended.at[:, lanes], mix_send.at[b], mix_recv.at[b], device(ey, dx)
        ), lanes

    def attend(b):
        is_left = b // (2 * SIDE)
        t = b - 2 * SIDE * is_left
        ey = jnp.where(is_left == 1, 2 * t, 2 * (t // SIDE))
        dx = jnp.where(is_left == 1, 0, lax.rem(SIDE - lax.rem(t, SIDE), SIDE))

        def at(dy):
            dy = lax.rem(dy, SIDE)
            return jnp.where(is_left == 1, dy, dy * SIDE + dx) * tile

        q = jnp.concatenate(
            [
                qkv[is_left, 0, rows(at(2 * SIDE - ey), tile), :],
                qkv[is_left, 0, rows(at(2 * SIDE - ey - 1) + half, half), :],
                qkv[is_left, 0, rows(at(2 * SIDE - ey + 1), half), :],
            ],
            axis=0,
        )
        chunk = min(KEY_CHUNK, keys)
        highest = jnp.full((2 * tile, HD), -jnp.inf, jnp.float32)
        for c in range(keys // chunk):
            s = lax.dot_general(
                q, qkv[is_left, 1, pl.ds(c * chunk, chunk), :], (((1,), (1,)), ((), ())),
                preferred_element_type=jnp.float32,
            )
            scores[:, c * chunk : (c + 1) * chunk] = s
            for g in range(chunk // HD):
                highest = jnp.maximum(highest, s[:, g * HD : (g + 1) * HD])
        top = jnp.max(highest, axis=1, keepdims=True)
        summed = jnp.zeros((2 * tile, HD), jnp.float32)
        total = jnp.zeros((2 * tile, HD), jnp.float32)
        for c in range(keys // chunk):
            p = jnp.exp2(scores[:, c * chunk : (c + 1) * chunk] - top)
            for g in range(chunk // HD):
                summed = summed + p[:, g * HD : (g + 1) * HD]
            total = total + jnp.dot(
                p.astype(jnp.bfloat16), qkv[is_left, 2, pl.ds(c * chunk, chunk), :],
                preferred_element_type=jnp.float32,
            )
        mixed[b] = (total / jnp.sum(summed, axis=1, keepdims=True)).astype(jnp.bfloat16)

    def attend_send(b):
        attend(b)
        mix_copy(b)[0].start()

    over(1, 2 * SIDE, attend_send)
    attend_send(2 * SIDE + 1)

    def attend_here(b):
        attend(b)
        attended[:, mix_copy(b)[1]] = mixed[b]

    def here(i):
        attend_here(i * 2 * SIDE)

    over(0, 2, here)

    over(1, 2 * SIDE, lambda b: mix_copy(b)[0].wait_recv())
    mix_copy(2 * SIDE + 1)[0].wait_recv()
    own_weight.wait()
    w_copy.wait_recv()

    wide_chunk = min(OUT_CHUNK, width)
    chunks = width // wide_chunk

    def cols_of(j):
        return pl.ds(pl.multiple_of(j * wide_chunk, HD), wide_chunk)

    def part_copy(d, j):
        here = part_out.at[pl.ds(d * half, half), cols_of(j)]
        there = part_in.at[pl.ds((1 - d) * half, half), cols_of(j)]
        return remote(
            here, there, part_send.at[d, j], part_recv.at[d, j], device(1 if d == 0 else SIDE - 1, 0)
        )

    depth = weight.shape[1]

    def project(j):
        cols = cols_of(j)
        r = jnp.dot(attended[:, :depth], weight[0, :, cols], preferred_element_type=jnp.float32)
        r = r + jnp.dot(attended[:, depth:], weight[1, :, cols], preferred_element_type=jnp.float32)
        part_out[:, cols] = r[tile:].astype(jnp.bfloat16)
        part_copy(0, j).start()
        part_copy(1, j).start()
        own[:, cols] = r[:tile]

    over(0, chunks, project)

    def finish(j):
        cols = cols_of(j)
        part_copy(0, j).wait_recv()
        part_copy(1, j).wait_recv()
        total = own[:, cols] + part_in[:, cols].astype(jnp.float32) + bias_ref[:, cols]
        out_ref[:, cols] = (gate_ref[:, cols] * total).astype(jnp.bfloat16)

    over(0, chunks, finish)

    over(1, SIDE, lambda dy: left_copy(dy).wait_send())
    over(1, CHIPS, lambda r: full_copy(r).wait_send())
    over(0, CHIPS, lambda r: pair_copy(r).wait_send())
    over(1, SIDE, lambda dx: row_copy(dx).wait_send())
    over(0, SIDE, lambda dx: pair_left_copy(dx).wait_send())
    w_copy.wait_send()
    over(1, 2 * SIDE, lambda b: mix_copy(b)[0].wait_send())
    mix_copy(2 * SIDE + 1)[0].wait_send()

    def sent(j):
        part_copy(0, j).wait_send()
        part_copy(1, j).wait_send()

    over(0, chunks, sent)


def body(q_in, k_in, v_in, q_gain, k_gain, out_weight, out_bias, out_gate):
    tile = q_in.shape[0]
    depth, width = out_weight.shape
    keys = 2 * CHIPS * tile
    chunks = width // min(OUT_CHUNK, width)
    vmem = pl.BlockSpec(memory_space=pltpu.VMEM)
    dma = pltpu.SemaphoreType.DMA
    return pl.pallas_call(
        kernel,
        out_shape=jax.ShapeDtypeStruct((tile, width), jnp.bfloat16),
        in_specs=[vmem] * 5 + [pl.BlockSpec(memory_space=pl.ANY)] + [vmem] * 2,
        out_specs=vmem,
        scratch_shapes=[
            pltpu.VMEM((3, HEADS, tile, HD), jnp.bfloat16),
            pltpu.VMEM((2, 3, keys, HD), jnp.bfloat16),
            pltpu.VMEM((2 * tile, keys), jnp.float32),
            pltpu.VMEM((CLASS_HEADS, 2 * tile, HD), jnp.bfloat16),
            pltpu.VMEM((2 * tile, CLASS_HEADS * HD), jnp.bfloat16),
            pltpu.VMEM((2, depth, width), jnp.bfloat16),
            pltpu.VMEM((tile, width), jnp.float32),
            pltpu.VMEM((tile, width), jnp.bfloat16),
            pltpu.VMEM((tile, width), jnp.bfloat16),
            dma((3,)),
            dma((CHIPS,)), dma((CHIPS,)),
            dma((SIDE,)), dma((SIDE,)),
            dma((SIDE,)), dma((SIDE,)),
            dma((CHIPS,)), dma((CHIPS,)),
            dma((SIDE,)), dma((SIDE,)),
            dma, dma,
            dma((CLASS_HEADS,)), dma((CLASS_HEADS,)),
            dma((2, chunks)), dma((2, chunks)),
        ],
        compiler_params=pltpu.CompilerParams(
            collective_id=0, has_side_effects=True, vmem_limit_bytes=60 * 1024 * 1024
        ),
        name="attention_branch",
    )(
        q_in, k_in, v_in, q_gain.reshape(1, -1), k_gain.reshape(1, -1), out_weight,
        out_bias.reshape(1, -1), out_gate.reshape(1, -1),
    )


def solution(mesh):
    split = P(("clip", "blk", "head"), None)
    in_specs = (split, split, split, P(), P(), P("head", None), P(), P())
    return jax.shard_map(body, mesh=mesh, in_specs=in_specs, out_specs=split, check_vma=False)
```

time: 361 us -> 85 us (0.24)
  waiting for transfers between devices: 188 us -> 0 us
  Pallas kernels: 0 us -> 79.7 us
  matrix products: 62.2 us -> 0 us
  local copies, waits for them, and re-layouts: 52.6 us -> 5.08 us
  blocking collectives: 27.5 us -> 0 us
  between operations: 13.2 us -> 0.01 us
  other arithmetic: 11.7 us -> 0 us
  starting transfers between devices: 4.53 us -> 0 us
    all_gather x2 -> x0, waiting for transfers between devices: 121 us -> none  [the longest x1 65.9 us: body(): value_piece = lax.all_gather(head_v, 'blk', axis=0, tiled=True)]
    pallas_call x0 -> x1, Pallas kernels: none -> 79.7 us  [body(): pl.pallas_call(kernel, out_shape=jax.ShapeDtypeStruct((tile, width), jnp....]
    dot_general x9 -> x0, matrix products: 62.2 us -> none  [the longest x4 26.7 us: block_step(): jnp.einsum('hrk,khd->rhd', weights.astype(jnp.bfloat16), value_block, pre...]
    reduce_scatter x1 -> x0, waiting for transfers between devices: 55.3 us -> none  [body(): lax.psum_scatter(jnp.dot(attended, out_weight, preferred_element_type=jnp...]
    all_to_all x2 -> x0, blocking collectives: 27.5 us -> none  [the longest x1 14.9 us: body(): lax.all_to_all(keys, 'head', split_axis=1, concat_axis=0, tiled=True)]
    another operation x2 -> x0, local copies, waits for them, and re-layouts: 25.2 us -> none  [the longest x1 12.6 us: body(): value_stack = value_three.reshape(length // 1024, 1024, head_count, HD)]
    unnamed x15 -> x1, local copies, waits for them, and re-layouts: 20.6 us -> 2.46 us
    all_to_all x1 -> x0, waiting for transfers between devices: 11.5 us -> none  [body(): lax.all_to_all(queries, 'head', split_axis=1, concat_axis=0, tiled=True)]
  transfers between devices with their start and end apart: 4 -> 0, of which waited for: 4 -> 0; matrix products, arithmetic and copies ran while one was open for 7% -> 0% of each run, Pallas kernels for 0% -> 0%
where the time goes in v1:
time: 85 us; the launch traced here: 84.8 us
  Pallas kernels  79.7 us (94%)
  local copies, waits for them, and re-layouts  5.08 us (6%)
    pallas_call x1, Pallas kernels, body(): pl.pallas_call(kernel, out_shape=jax.ShapeDtypeStruct((tile, width), jnp....  79.7 us
    unnamed x1, local copies, waits for them, and re-layouts  2.46 us

profile of v1, /device:TPU:1, one launch (start us, length us, event | category | flops | bytes accessed | tf_op | source)
XLA Modules:
  0.0 84.8 jit_solution(15227739861932033242)
XLA Ops:
  0.0 1.3 %reshape.12.qg_ref = f32[1,2560]{1,0:T(1,128)} reshape(f32[2560]{0:T(1024)} %param.11) | data formatting | bytes 20480 | tf_op jit(solution)/shard_map/reshape | solution.py:322
  1.3 1.3 %reshape.13.kg_ref = f32[1,2560]{1,0:T(1,128)} reshape(f32[2560]{0:T(1024)} %param.12) | data formatting | bytes 20480 | tf_op jit(solution)/shard_map/reshape | solution.py:322
  2.6 79.7 %attention_branch.1 = bf16[128,5120]{1,0:T(8,128)(2,1)} custom-call(bf16[128,2560]{1,0:T(8,128)(2,1)} %q_ref.1, bf16[128,2560]{1,0:T(8,128)(2,1)} %k_ref.1, bf16[128,2560]{1,0:T(8,128)(2,1)} %v_ref.1, f32[1,2560]{1,0:T(1,128)} %reshape.12.qg_ref, f32[1,2560]{1,0:T(1,128)} %reshape.13.kg_ref, bf16[640,5120]{1,0:T(8,128)(2,1)} %w_ref.1, f32[1,5120]{1,0:T(1,128)} %bitcast.2, ...), custom_call_target="tpu_custom_call" | custom-call | tf_op jit(solution)/shard_map/attention_branch/pallas_call | solution.py:292
  82.3 2.5 %copy.10 = bf16[128,5120]{1,0:T(8,128)(2,1)} copy(bf16[128,5120]{1,0:T(8,128)(2,1)} %attention_branch.1) | data formatting | bytes 2621440

commit v2 on v1

--- a/solution.py
+++ b/solution.py
@@ -21,7 +21,7 @@
 def kernel(
     q_ref, k_ref, v_ref, qg_ref, kg_ref, w_ref, bias_ref, gate_ref, out_ref,
     stage, qkv, scores, mixed, attended, weight, own, part_out, part_in,
-    local_sem, full_send, full_recv, left_send, left_recv, row_send, row_recv,
+    local_sem, full_send, full_recv, left_send, left_recv, row_send, row_recv, relay_send, relay_recv,
     pair_send, pair_recv, pair_left_send, pair_left_recv, w_send, w_recv,
     mix_send, mix_recv, part_send, part_recv,
 ):
@@ -76,7 +76,9 @@
         factor = lax.rsqrt(jnp.mean(wide * wide, axis=-1, keepdims=True) + 1e-06)
         for h in range(HEADS):
             cols = slice(h * HD, (h + 1) * HD)
-            gain = gain_ref[:, cols] * scale if scale is not None else gain_ref[:, cols]
+            gain = gain_ref[cols].reshape(1, HD)
+            if scale is not None:
+                gain = gain * scale
             stage[which, h] = (ref[:, cols].astype(jnp.float32) * factor * gain).astype(jnp.bfloat16)
 
     normalize(q_ref, qg_ref, 0, HD ** (-0.5) * math.log2(math.e))
@@ -109,15 +111,26 @@
         there = qkv.at[0, pl.ds(1, 2), rows((CHIPS + r) * tile, tile), :]
         return remote(here, there, pair_send.at[r], pair_recv.at[r], sibling)
 
-    def row_copy(dx):
-        here = qkv.at[1, pl.ds(1, 2), rows(0, SIDE * tile), :]
-        there = qkv.at[1, pl.ds(1, 2), rows(dx * SIDE * tile, SIDE * tile), :]
-        return remote(here, there, row_send.at[dx], row_recv.at[dx], device(0, dx))
-
-    def pair_left_copy(dx):
-        here = qkv.at[1, pl.ds(1, 2), rows(dx * SIDE * tile, SIDE * tile), :]
-        there = qkv.at[1, pl.ds(1, 2), rows((CHIPS + dx * SIDE) * tile, SIDE * tile), :]
-        return remote(here, there, pair_left_send.at[dx], pair_left_recv.at[dx], sibling)
+    def left_rows(i):
+        return qkv.at[1, pl.ds(1, 2), rows(i * tile, tile), :]
+
+    def row_copy(d, t):
+        dx = 1 + 2 * d
+        return remote(
+            left_rows(t), left_rows(dx * SIDE + t), row_send.at[d, t], row_recv.at[d, t], device(0, dx)
+        )
+
+    def relay_copy(t):
+        dx = 1 + 2 * (t // 2)
+        return remote(
+            left_rows(dx * SIDE + t), left_rows(2 * SIDE + t), relay_send.at[t], relay_recv.at[t],
+            device(0, dx),
+        )
+
+    def pair_left_copy(i):
+        return remote(
+            left_rows(i), left_rows(CHIPS + i), pair_left_send.at[i], pair_left_recv.at[i], sibling
+        )
 
     def over(first, last, act):
         def step(i, carry):
@@ -126,8 +139,8 @@
 
         lax.fori_loop(first, last, step, 0)
 
+    over(1, CHIPS, lambda r: full_copy(r).start())
     over(1, SIDE, lambda dy: left_copy(dy).start())
-    over(1, CHIPS, lambda r: full_copy(r).start())
     own_full = pltpu.make_async_copy(
         stage.at[:, full_head(y, x)], qkv.at[0, :, pl.ds(0, tile), :], local_sem.at[0]
     )
@@ -140,58 +153,61 @@
     own_left.wait()
     pair_copy(0).start()
 
-    over(1, SIDE, lambda dy: left_copy(dy).wait_recv())
-    over(1, SIDE, lambda dx: row_copy(dx).start())
-    pair_left_copy(0).start()
-
     def pass_on(r):
         full_copy(r).wait_recv()
         pair_copy(r).start()
 
     over(1, CHIPS, pass_on)
 
-    def pass_on_left(dx):
-        row_copy(dx).wait_recv()
-        pair_left_copy(dx).start()
-
-    over(1, SIDE, pass_on_left)
+    def spread_left(t):
+        row_copy(0, t).start()
+        row_copy(1, t).start()
+        pair_left_copy(t).start()
+
+    spread_left(0)
     over(0, CHIPS, lambda r: pair_copy(r).wait_recv())
-    over(0, SIDE, lambda dx: pair_left_copy(dx).wait_recv())
-
-    def mix_copy(b):
-        is_left = b // (2 * SIDE)
-        t = b - 2 * SIDE * is_left
-        ey = jnp.where(is_left == 1, 2 * t, 2 * (t // SIDE))
-        dx = jnp.where(is_left == 1, 0, lax.rem(t, SIDE))
-        slot = jnp.where(is_left == 1, 2 * SIDE + y // 2, SIDE * (y // 2) + x)
+
+    def target(is_left, u, i):
+        if is_left:
+            return 2 * i, 0, 2 * SIDE + i, 2 * SIDE + y // 2
+        ey, dx = 2 * (u // 2), 2 * lax.rem(u, 2) + i
+        return ey, dx, (ey // 2) * SIDE + dx, SIDE * (y // 2) + x
+
+    def mix_place(is_left, slot, rnd):
         lanes = pl.ds(pl.multiple_of(slot * HD, HD), HD)
-        return remote(
-            mixed.at[b], attended.at[:, lanes], mix_send.at[b], mix_recv.at[b], device(ey, dx)
-        ), lanes
-
-    def attend(b):
-        is_left = b // (2 * SIDE)
-        t = b - 2 * SIDE * is_left
-        ey = jnp.where(is_left == 1, 2 * t, 2 * (t // SIDE))
-        dx = jnp.where(is_left == 1, 0, lax.rem(SIDE - lax.rem(t, SIDE), SIDE))
-
-        def at(dy):
-            dy = lax.rem(dy, SIDE)
-            return jnp.where(is_left == 1, dy, dy * SIDE + dx) * tile
-
-        q = jnp.concatenate(
-            [
-                qkv[is_left, 0, rows(at(2 * SIDE - ey), tile), :],
-                qkv[is_left, 0, rows(at(2 * SIDE - ey - 1) + half, half), :],
-                qkv[is_left, 0, rows(at(2 * SIDE - ey + 1), half), :],
-            ],
-            axis=0,
-        )
+        return pl.ds((1 - rnd) * tile, tile), lanes
+
+    def mix_copy(rnd, is_left, u, i):
+        ey, dx, t, slot = target(is_left, u, i)
+        place = mix_place(is_left, slot, rnd)
+        return remote(
+            mixed.at[rnd, t], attended.at[place[0], place[1]], mix_send.at[rnd, t], mix_recv.at[rnd, t],
+            device(ey, dx),
+        )
+
+    def attend(rnd, is_left, u):
+        which = 1 if is_left else 0
+        pieces = []
+        for i in range(2):
+            ey, dx, _, _ = target(is_left, u, i)
+
+            def at(dy):
+                dy = lax.rem(dy, SIDE)
+                return (dy if is_left else dy * SIDE + lax.rem(SIDE - dx, SIDE)) * tile
+
+            if rnd == 0:
+                pieces += [
+                    qkv[which, 0, rows(at(2 * SIDE - ey - 1) + half, half), :],
+                    qkv[which, 0, rows(at(2 * SIDE - ey + 1), half), :],
+                ]
+            else:
+                pieces.append(qkv[which, 0, rows(at(2 * SIDE - ey), tile), :])
+        q = jnp.concatenate(pieces, axis=0)
         chunk = min(KEY_CHUNK, keys)
         highest = jnp.full((2 * tile, HD), -jnp.inf, jnp.float32)
         for c in range(keys // chunk):
             s = lax.dot_general(
-                q, qkv[is_left, 1, pl.ds(c * chunk, chunk), :], (((1,), (1,)), ((), ())),
+                q, qkv[which, 1, pl.ds(c * chunk, chunk), :], (((1,), (1,)), ((), ())),
                 preferred_element_type=jnp.float32,
             )
             scores[:, c * chunk : (c + 1) * chunk] = s
@@ -205,31 +221,61 @@
             for g in range(chunk // HD):
                 summed = summed + p[:, g * HD : (g + 1) * HD]
             total = total + jnp.dot(
-                p.astype(jnp.bfloat16), qkv[is_left, 2, pl.ds(c * chunk, chunk), :],
+                p.astype(jnp.bfloat16), qkv[which, 2, pl.ds(c * chunk, chunk), :],
                 preferred_element_type=jnp.float32,
             )
-        mixed[b] = (total / jnp.sum(summed, axis=1, keepdims=True)).astype(jnp.bfloat16)
-
-    def attend_send(b):
-        attend(b)
-        mix_copy(b)[0].start()
-
-    over(1, 2 * SIDE, attend_send)
-    attend_send(2 * SIDE + 1)
-
-    def attend_here(b):
-        attend(b)
-        attended[:, mix_copy(b)[1]] = mixed[b]
-
-    def here(i):
-        attend_here(i * 2 * SIDE)
-
-    over(0, 2, here)
-
-    over(1, 2 * SIDE, lambda b: mix_copy(b)[0].wait_recv())
-    mix_copy(2 * SIDE + 1)[0].wait_recv()
+        result = (total / jnp.sum(summed, axis=1, keepdims=True)).astype(jnp.bfloat16)
+        for i in range(2):
+            _, _, t, slot = target(is_left, u, i)
+            mixed[rnd, t] = result[i * tile : (i + 1) * tile]
+
+        def keep():
+            place = mix_place(is_left, target(is_left, u, 0)[3], rnd)
+            attended[place[0], place[1]] = result[:tile]
+
+        if is_left:
+            keep()
+        else:
+            pl.when(u == 0)(keep)
+            pl.when(u > 0)(lambda: mix_copy(rnd, is_left, u, 0).start())
+        mix_copy(rnd, is_left, u, 1).start()
+
+    def first_round(u):
+        attend(0, False, u)
+
+        @pl.when(u > 0)
+        def _():
+            left_copy(u).wait_recv()
+            spread_left(u)
+
+    over(0, SIDE, first_round)
+
+    def second_round(u):
+        row_copy(0, u).wait_recv()
+        row_copy(1, u).wait_recv()
+        relay_copy(u).start()
+        pair_left_copy(SIDE + u).start()
+        pair_left_copy(3 * SIDE + u).start()
+        attend(1, False, u)
+
+    over(0, SIDE, second_round)
+
+    def end_left(t):
+        relay_copy(t).wait_recv()
+        pair_left_copy(2 * SIDE + t).start()
+
+    over(0, SIDE, end_left)
+    over(0, CHIPS, lambda i: pair_left_copy(i).wait_recv())
     own_weight.wait()
     w_copy.wait_recv()
+
+    def mix_wait(rnd):
+        def full(u):
+            pl.when(u > 0)(lambda: mix_copy(rnd, False, u, 0).wait_recv())
+            mix_copy(rnd, False, u, 1).wait_recv()
+
+        over(0, SIDE, full)
+        mix_copy(rnd, True, 0, 1).wait_recv()
 
     wide_chunk = min(OUT_CHUNK, width)
     chunks = width // wide_chunk
@@ -246,16 +292,26 @@
 
     depth = weight.shape[1]
 
-    def project(j):
+    def product(at, cols):
+        r = jnp.dot(attended[at, :depth], weight[0, :, cols], preferred_element_type=jnp.float32)
+        return r + jnp.dot(attended[at, depth:], weight[1, :, cols], preferred_element_type=jnp.float32)
+
+    def project_sent(j):
         cols = cols_of(j)
-        r = jnp.dot(attended[:, :depth], weight[0, :, cols], preferred_element_type=jnp.float32)
-        r = r + jnp.dot(attended[:, depth:], weight[1, :, cols], preferred_element_type=jnp.float32)
-        part_out[:, cols] = r[tile:].astype(jnp.bfloat16)
+        part_out[:, cols] = product(pl.ds(tile, tile), cols).astype(jnp.bfloat16)
         part_copy(0, j).start()
         part_copy(1, j).start()
-        own[:, cols] = r[:tile]
-
-    over(0, chunks, project)
+
+    def project_kept(j):
+        cols = cols_of(j)
+        own[:, cols] = product(pl.ds(0, tile), cols)
+
+    attend(0, True, 0)
+    attend(1, True, 0)
+    mix_wait(0)
+    over(0, chunks, project_sent)
+    mix_wait(1)
+    over(0, chunks, project_kept)
 
     def finish(j):
         cols = cols_of(j)
@@ -269,11 +325,23 @@
     over(1, SIDE, lambda dy: left_copy(dy).wait_send())
     over(1, CHIPS, lambda r: full_copy(r).wait_send())
     over(0, CHIPS, lambda r: pair_copy(r).wait_send())
-    over(1, SIDE, lambda dx: row_copy(dx).wait_send())
-    over(0, SIDE, lambda dx: pair_left_copy(dx).wait_send())
+
+    def row_sent(t):
+        row_copy(0, t).wait_send()
+        row_copy(1, t).wait_send()
+        relay_copy(t).wait_send()
+
+    over(0, SIDE, row_sent)
+    over(0, CHIPS, lambda i: pair_left_copy(i).wait_send())
     w_copy.wait_send()
-    over(1, 2 * SIDE, lambda b: mix_copy(b)[0].wait_send())
-    mix_copy(2 * SIDE + 1)[0].wait_send()
+    for rnd in range(2):
+
+        def mix_sent(u, rnd=rnd):
+            pl.when(u > 0)(lambda: mix_copy(rnd, False, u, 0).wait_send())
+            mix_copy(rnd, False, u, 1).wait_send()
+
+        over(0, SIDE, mix_sent)
+        mix_copy(rnd, True, 0, 1).wait_send()
 
     def sent(j):
         part_copy(0, j).wait_send()
@@ -291,14 +359,14 @@
     dma = pltpu.SemaphoreType.DMA
     return pl.pallas_call(
         kernel,
-        out_shape=jax.ShapeDtypeStruct((tile, width), jnp.bfloat16),
+        out_shape=pltpu.VMEM((tile, width), jnp.bfloat16),
         in_specs=[vmem] * 5 + [pl.BlockSpec(memory_space=pl.ANY)] + [vmem] * 2,
         out_specs=vmem,
         scratch_shapes=[
             pltpu.VMEM((3, HEADS, tile, HD), jnp.bfloat16),
             pltpu.VMEM((2, 3, keys, HD), jnp.bfloat16),
             pltpu.VMEM((2 * tile, keys), jnp.float32),
-            pltpu.VMEM((CLASS_HEADS, 2 * tile, HD), jnp.bfloat16),
+            pltpu.VMEM((2, CLASS_HEADS, tile, HD), jnp.bfloat16),
             pltpu.VMEM((2 * tile, CLASS_HEADS * HD), jnp.bfloat16),
             pltpu.VMEM((2, depth, width), jnp.bfloat16),
             pltpu.VMEM((tile, width), jnp.float32),
@@ -307,11 +375,12 @@
             dma((3,)),
             dma((CHIPS,)), dma((CHIPS,)),
             dma((SIDE,)), dma((SIDE,)),
+            dma((2, SIDE)), dma((2, SIDE)),
             dma((SIDE,)), dma((SIDE,)),
             dma((CHIPS,)), dma((CHIPS,)),
-            dma((SIDE,)), dma((SIDE,)),
+            dma((CHIPS,)), dma((CHIPS,)),
             dma, dma,
-            dma((CLASS_HEADS,)), dma((CLASS_HEADS,)),
+            dma((2, CLASS_HEADS)), dma((2, CLASS_HEADS)),
             dma((2, chunks)), dma((2, chunks)),
         ],
         compiler_params=pltpu.CompilerParams(
@@ -319,7 +388,7 @@
         ),
         name="attention_branch",
     )(
-        q_in, k_in, v_in, q_gain.reshape(1, -1), k_gain.reshape(1, -1), out_weight,
+        q_in, k_in, v_in, q_gain, k_gain, out_weight,
         out_bias.reshape(1, -1), out_gate.reshape(1, -1),
     )
 

time: 85 us -> 73.8 us (0.87); the launches traced: 84.8 us -> 72.7 us
  Pallas kernels: 79.7 us -> 71.6 us
  local copies, waits for them, and re-layouts: 5.08 us -> 1.06 us
    pallas_call x1, Pallas kernels: 79.7 us -> 71.6 us  [body(): pl.pallas_call(kernel, out_shape=pltpu.VMEM((tile, width), jnp.bfloat16),...]
    reshape x2 -> x0, local copies, waits for them, and re-layouts: 2.62 us -> none  [the longest x1 1.31 us: body(): q_gain.reshape(1, -1)]
    unnamed x1, local copies, waits for them, and re-layouts: 2.46 us -> 1.06 us
where the time goes in v2:
time: 73.8 us; the launch traced here: 72.7 us
  Pallas kernels  71.6 us (97%)
  local copies, waits for them, and re-layouts  1.06 us (1%)
    pallas_call x1, Pallas kernels, body(): pl.pallas_call(kernel, out_shape=pltpu.VMEM((tile, width), jnp.bfloat16),...  71.6 us

profile of v2, /device:TPU:1, one launch (start us, length us, event | category | flops | bytes accessed | tf_op | source)
XLA Modules:
  0.0 72.7 jit_solution(13643748264801717707)
XLA Ops:
  0.0 71.6 %attention_branch.1 = bf16[128,5120]{1,0:T(8,128)(2,1)S(1)} custom-call(bf16[128,2560]{1,0:T(8,128)(2,1)} %q_ref.1, bf16[128,2560]{1,0:T(8,128)(2,1)} %k_ref.1, bf16[128,2560]{1,0:T(8,128)(2,1)} %v_ref.1, f32[2560]{0:T(1024)} %qg_ref.1, f32[2560]{0:T(1024)} %kg_ref.1, bf16[640,5120]{1,0:T(8,128)(2,1)} %w_ref.1, f32[1,5120]{1,0:T(1,128)} %bitcast.2, ...), custom_call_target="tpu_custom_call" | custom-call | tf_op jit(solution)/shard_map/attention_branch/pallas_call | solution.py:360
  71.6 1.1 %copy.10 = bf16[128,5120]{1,0:T(8,128)(2,1)} copy(bf16[128,5120]{1,0:T(8,128)(2,1)S(1)} %attention_branch.1) | data formatting | bytes 2621440

commit v3 on v2

v3 whole, which is shorter than its diff:
```python
import functools
import math

import jax
import jax.numpy as jnp
from jax import lax
from jax.experimental import pallas as pl
from jax.experimental.pallas import tpu as pltpu
from jax.sharding import PartitionSpec as P

HD = 128
SIDE = 4
CHIPS = SIDE * SIDE
CLASS_HEADS = 10
HEADS = 20
KEY_CHUNK = 512
OUT_CHUNK = 1024
MESH = pl.DeviceIdType.MESH


def hops(r):
    dy, dx = r // SIDE, r % SIDE
    return min(dy, SIDE - dy) + min(dx, SIDE - dx)


FAR = sorted(range(1, CHIPS), key=lambda r: -hops(r))
LATE = [r for r in FAR if r // SIDE % 2 == 0]


def kernel(
    q_ref, k_ref, v_ref, qg_ref, kg_ref, w_ref, bias_ref, gate_ref, out_ref,
    stage, qkv, scores, mixed, attended, left_mixed, left_attended, weight, other, own, part_out, part_in,
    local_sem, full_send, full_recv, late_send, late_recv, left_send, left_recv, row_send, row_recv, relay_send, relay_recv,
    pair_send, pair_recv, pair_left_send, pair_left_recv, w_send, w_recv,
    near_send, near_recv, ring_send, ring_recv, other_send, other_recv, left_mix_send, left_mix_recv,
    mix_send, mix_recv, part_send, part_recv,
):
    tile = q_ref.shape[0]
    half = tile // 2
    keys = 2 * CHIPS * tile
    width = out_ref.shape[1]
    blk, head, z = lax.axis_index("blk"), lax.axis_index("head"), lax.axis_index("clip")
    clips = lax.axis_size("clip")
    depth = w_ref.shape[0]
    left_row = 2 * SIDE * HD - depth
    piece = HD // clips
    x, core = lax.rem(blk, SIDE), lax.rem(head, 2)
    y = 2 * (blk // SIDE) + head // 2

    def chip(dy, dx):
        return lax.rem(y + dy, SIDE), lax.rem(x + dx, SIDE)

    def device(dy, dx):
        yy, xx = chip(dy, dx)
        return {"blk": (yy // 2) * SIDE + xx, "head": lax.rem(yy, 2) * 2 + core}

    sibling = {"blk": blk, "head": (head // 2) * 2 + 1 - core}

    def full_head(yy, xx):
        return CLASS_HEADS * lax.rem(yy, 2) + SIDE * (yy // 2) + xx

    def left_head(yy):
        return CLASS_HEADS * lax.rem(yy, 2) + 2 * SIDE + yy // 2

    def rows(start, size):
        return pl.ds(pl.multiple_of(start, half), size)

    def remote(src, dst, send, recv, target):
        return pltpu.make_async_remote_copy(
            src_ref=src, dst_ref=dst, send_sem=send, recv_sem=recv,
            device_id=target, device_id_type=MESH,
        )

    own_weight = pltpu.make_async_copy(w_ref, weight.at[core], local_sem.at[2])
    own_weight.start()

    barrier = pltpu.get_barrier_semaphore()

    def greet(r, carry):
        pl.semaphore_signal(
            barrier, inc=1, device_id=device(r // SIDE, lax.rem(r, SIDE)), device_id_type=MESH
        )
        return carry

    lax.fori_loop(1, CHIPS, greet, 0)

    def clip_at(dz):
        return {"clip": lax.rem(z + dz, clips), "blk": blk, "head": head}

    beside = [1, clips - 1] if clips > 2 else [1][: clips - 1]
    for dz in beside:
        pl.semaphore_signal(barrier, inc=1, device_id=clip_at(dz), device_id_type=MESH)
    pl.semaphore_signal(barrier, inc=1, device_id=sibling, device_id_type=MESH)

    def normalize(ref, gain_ref, which, scale):
        wide = ref[...].astype(jnp.float32)
        factor = lax.rsqrt(jnp.mean(wide * wide, axis=-1, keepdims=True) + 1e-06)
        for h in range(HEADS):
            cols = slice(h * HD, (h + 1) * HD)
            gain = gain_ref[cols].reshape(1, HD)
            if scale is not None:
                gain = gain * scale
            stage[which, h] = (ref[:, cols].astype(jnp.float32) * factor * gain).astype(jnp.bfloat16)

    normalize(q_ref, qg_ref, 0, HD ** (-0.5) * math.log2(math.e))
    normalize(k_ref, kg_ref, 1, None)
    for h in range(HEADS):
        stage[2, h] = v_ref[:, h * HD : (h + 1) * HD].T

    pl.semaphore_wait(barrier, CHIPS + len(beside))

    w_copy = remote(w_ref, weight.at[core], w_send, w_recv, sibling)
    w_copy.start()

    def near_copy(d):
        start = z * 2 * piece + d * piece
        return remote(
            w_ref.at[pl.ds(pl.multiple_of(left_row + start, piece), piece)],
            other.at[pl.ds(pl.multiple_of(start, piece), piece)],
            near_send.at[d], near_recv.at[d], device(1 + 2 * d, 0),
        )

    def slice_of(origin):
        return other.at[pl.ds(pl.multiple_of(origin * 2 * piece, 2 * piece), 2 * piece)]

    def origin_of(d, step):
        return lax.rem(z + (clips - step if d == 0 else step), clips)

    def ring_copy(d, step):
        moved = slice_of(origin_of(d, step - 1))
        return remote(
            moved, moved, ring_send.at[d, step], ring_recv.at[d, step], clip_at(1 if d == 0 else clips - 1)
        )

    def other_copy(origin):
        return remote(
            slice_of(origin), slice_of(origin), other_send.at[origin], other_recv.at[origin], sibling
        )

    ring_steps = [clips // 2, (clips - 1) // 2]

    def ring(step):
        @pl.when(core == 1)
        def _():
            if step == 1:
                near_copy(0).wait_recv()
                near_copy(1).wait_recv()
                other_copy(z).start()
            for d in range(2):
                if 1 < step <= ring_steps[d] + 1:
                    ring_copy(d, step - 1).wait_recv()
                    other_copy(origin_of(d, step - 1)).start()
                if step <= ring_steps[d]:
                    ring_copy(d, step).start()

    def left_copy(dy):
        yy, xx = chip(dy, 0)
        return remote(
            stage.at[:, left_head(yy)], qkv.at[1, :, rows(dy * tile, tile), :],
            left_send.at[dy], left_recv.at[dy], device(dy, 0),
        )

    def full_copy(r):
        dy, dx = r // SIDE, r % SIDE
        first = 1 if dy % 2 == 0 else 0
        return remote(
            stage.at[pl.ds(first, 3 - first), full_head(*chip(dy, dx))],
            qkv.at[0, pl.ds(first, 3 - first), rows(r * tile, tile), :],
            full_send.at[r], full_recv.at[r], device(dy, dx),
        )

    def late_copy(r):
        dy, dx = r // SIDE, r % SIDE
        return remote(
            stage.at[0, full_head(*chip(dy, dx))], qkv.at[0, 0, rows(r * tile, tile), :],
            late_send.at[r], late_recv.at[r], device(dy, dx),
        )

    def pair_copy(r):
        here = qkv.at[0, pl.ds(1, 2), rows(r * tile, tile), :]
        there = qkv.at[0, pl.ds(1, 2), rows((CHIPS + r) * tile, tile), :]
        return remote(here, there, pair_send.at[r], pair_recv.at[r], sibling)

    def left_rows(i):
        return qkv.at[1, pl.ds(1, 2), rows(i * tile, tile), :]

    def row_copy(d, t):
        dx = 1 + 2 * d
        return remote(
            left_rows(t), left_rows(dx * SIDE + t), row_send.at[d, t], row_recv.at[d, t], device(0, dx)
        )

    def relay_copy(t):
        dx = 1 + 2 * (t // 2)
        return remote(
            left_rows(dx * SIDE + t), left_rows(2 * SIDE + t), relay_send.at[t], relay_recv.at[t],
            device(0, dx),
        )

    def pair_left_copy(i):
        return remote(
            left_rows(i), left_rows(CHIPS + i), pair_left_send.at[i], pair_left_recv.at[i], sibling
        )

    def over(first, last, act):
        def step(i, carry):
            act(i)
            return carry

        lax.fori_loop(first, last, step, 0)

    @pl.when(core == 1)
    def _():
        near_copy(0).start()
        near_copy(1).start()

    for r in FAR:
        full_copy(r).start()
    over(1, SIDE, lambda dy: left_copy(dy).start())
    for r in LATE:
        late_copy(r).start()
    own_full = pltpu.make_async_copy(
        stage.at[:, full_head(y, x)], qkv.at[0, :, pl.ds(0, tile), :], local_sem.at[0]
    )
    own_left = pltpu.make_async_copy(
        stage.at[:, left_head(y)], qkv.at[1, :, pl.ds(0, tile), :], local_sem.at[1]
    )
    own_full.start()
    own_left.start()
    own_full.wait()
    own_left.wait()
    pair_copy(0).start()

    def pass_on(r):
        full_copy(r).wait_recv()
        pair_copy(r).start()

    for r in FAR:
        pass_on(r)

    def spread_left(t):
        row_copy(0, t).start()
        row_copy(1, t).start()
        pair_left_copy(t).start()

    spread_left(0)
    over(0, CHIPS, lambda r: pair_copy(r).wait_recv())

    def softmax_rows(which, q):
        count = q.shape[0]
        chunk = min(KEY_CHUNK, keys)
        highest = jnp.full((8, count), -jnp.inf, jnp.float32)
        for c in range(keys // chunk):
            s = lax.dot_general(
                qkv[which, 1, pl.ds(c * chunk, chunk), :], q, (((1,), (1,)), ((), ())),
                preferred_element_type=jnp.float32,
            )
            scores[c * chunk : (c + 1) * chunk, :] = s
            highest = jnp.maximum(highest, jnp.max(s.reshape(chunk // 8, 8, count), axis=0))
        top = jnp.max(highest, axis=0, keepdims=True)
        summed = jnp.zeros((8, count), jnp.float32)
        total = jnp.zeros((HD, count), jnp.float32)
        for c in range(keys // chunk):
            p = jnp.exp2(scores[c * chunk : (c + 1) * chunk, :] - top)
            summed = summed + jnp.sum(p.reshape(chunk // 8, 8, count), axis=0)
            values = jnp.concatenate(
                [qkv[which, 2, pl.ds(k * tile, tile), :] for k in range(c * chunk // tile, (c + 1) * chunk // tile)],
                axis=1,
            )
            total = total + jnp.dot(values, p.astype(jnp.bfloat16), preferred_element_type=jnp.float32)
        return (total / jnp.sum(summed, axis=0, keepdims=True)).T.astype(jnp.bfloat16)

    def lanes_of(slot):
        return pl.ds(pl.multiple_of(slot * HD, HD), HD)

    def mix_place(rnd):
        return pl.ds((1 - rnd) * tile, tile), lanes_of(SIDE * (y // 2) + x)

    def mix_copy(rnd, ey, dx):
        place, t = mix_place(rnd), (ey // 2) * SIDE + dx
        return remote(
            mixed.at[rnd, t], attended.at[place[0], place[1]], mix_send.at[rnd, t], mix_recv.at[rnd, t],
            device(ey, dx),
        )

    def attend(rnd, ey):
        pieces = []
        for dx in range(SIDE):

            def at(dy):
                return (lax.rem(dy, SIDE) * SIDE + (SIDE - dx) % SIDE) * tile

            if rnd == 0:
                pieces += [
                    qkv[0, 0, rows(at(2 * SIDE - ey - 1) + half, half), :],
                    qkv[0, 0, rows(at(2 * SIDE - ey + 1), half), :],
                ]
            else:
                pieces.append(qkv[0, 0, rows(at(2 * SIDE - ey), tile), :])
        result = softmax_rows(0, jnp.concatenate(pieces, axis=0))
        for dx in range(SIDE):
            mixed[rnd, (ey // 2) * SIDE + dx] = result[dx * tile : (dx + 1) * tile]

        @pl.when(ey == 0)
        def _():
            place = mix_place(rnd)
            attended[place[0], place[1]] = result[:tile]

        pl.when(ey > 0)(lambda: mix_copy(rnd, ey, 0).start())
        for dx in (2, 1, 3):
            mix_copy(rnd, ey, dx).start()

    def left_place(dy):
        return lanes_of(y // 2 + 2 * (dy & 1 if isinstance(dy, int) else lax.rem(dy, 2)))

    def left_mix_copy(dy):
        return remote(
            left_mixed.at[dy], left_attended.at[:, left_place(dy)], left_mix_send.at[dy],
            left_mix_recv.at[dy], device(SIDE - dy, 0),
        )

    def attend_left():
        result = softmax_rows(1, qkv[1, 0, pl.ds(0, SIDE * tile), :])
        left_attended[:, left_place(0)] = result[:tile]
        for dy in (2, 1, 3):
            left_mixed[dy] = result[dy * tile : (dy + 1) * tile]
            left_mix_copy(dy).start()

    def mix_wait(rnd):
        def full(t):
            mix_copy(rnd, 2 * (t // SIDE), lax.rem(t, SIDE)).wait_recv()

        over(1, 2 * SIDE, full)

    def take_left(u):
        left_copy(u).wait_recv()
        spread_left(u)

    def relay_left(u):
        row_copy(0, u).wait_recv()
        row_copy(1, u).wait_recv()
        relay_copy(u).start()
        pair_left_copy(SIDE + u).start()
        pair_left_copy(3 * SIDE + u).start()

    def end_left(t):
        relay_copy(t).wait_recv()
        pair_left_copy(2 * SIDE + t).start()

    ring(1)
    over(0, 2, lambda i: attend(0, 2 - 2 * i))
    over(1, SIDE, take_left)
    ring(2)
    for r in LATE:
        late_copy(r).wait_recv()
    attend(1, 2)

    wide_chunk = min(OUT_CHUNK, width)
    chunks = width // wide_chunk

    def cols_of(j):
        return pl.ds(pl.multiple_of(j * wide_chunk, HD), wide_chunk)

    def part_copy(d, j):
        here = part_out.at[pl.ds(d * half, half), cols_of(j)]
        there = part_in.at[pl.ds((1 - d) * half, half), cols_of(j)]
        return remote(
            here, there, part_send.at[d, j], part_recv.at[d, j], device(1 if d == 0 else SIDE - 1, 0)
        )

    def dot(a, b):
        return jnp.dot(a, b, preferred_element_type=jnp.float32)

    def product(at, cols):
        r = dot(attended[at, :depth], weight[0, :, cols])
        return r + dot(attended[at, depth:], weight[1, :left_row, cols])

    def project_sent(j):
        cols = cols_of(j)
        part_out[:, cols] = product(pl.ds(tile, tile), cols).astype(jnp.bfloat16)
        part_copy(0, j).start()
        part_copy(1, j).start()

    def project_kept(j):
        cols = cols_of(j)
        own[:, cols] = product(pl.ds(0, tile), cols)

    own_weight.wait()
    w_copy.wait_recv()
    mix_wait(0)
    over(0, chunks, project_sent)
    ring(3)
    attend(1, 0)
    over(0, SIDE, relay_left)
    ring(4)
    mix_wait(1)
    over(0, chunks, project_kept)
    over(0, SIDE, end_left)
    over(0, CHIPS, lambda i: pair_left_copy(i).wait_recv())
    attend_left()
    ring(5)
    over(1, SIDE, lambda dy: left_mix_copy(dy).wait_recv())

    @pl.when(core == 0)
    def _():
        over(0, clips, lambda origin: other_copy(origin).wait_recv())


    def finish(j):
        cols = cols_of(j)
        r = dot(left_attended[:, : 2 * HD], weight[1, left_row:, cols])
        r = r + dot(left_attended[:, 2 * HD :], other[:, cols])
        part_copy(0, j).wait_recv()
        part_copy(1, j).wait_recv()
        total = own[:, cols] + r + part_in[:, cols].astype(jnp.float32) + bias_ref[:, cols]
        out_ref[:, cols] = (gate_ref[:, cols] * total).astype(jnp.bfloat16)

    over(0, chunks, finish)

    over(1, SIDE, lambda dy: left_copy(dy).wait_send())
    for r in FAR:
        full_copy(r).wait_send()
    for r in LATE:
        late_copy(r).wait_send()
    over(0, CHIPS, lambda r: pair_copy(r).wait_send())

    def row_sent(t):
        row_copy(0, t).wait_send()
        row_copy(1, t).wait_send()
        relay_copy(t).wait_send()

    over(0, SIDE, row_sent)
    over(0, CHIPS, lambda i: pair_left_copy(i).wait_send())
    w_copy.wait_send()
    over(1, SIDE, lambda dy: left_mix_copy(dy).wait_send())

    @pl.when(core == 1)
    def _():
        near_copy(0).wait_send()
        near_copy(1).wait_send()
        for d in range(2):
            for step in range(1, ring_steps[d] + 1):
                ring_copy(d, step).wait_send()
        over(0, clips, lambda origin: other_copy(origin).wait_send())

    for rnd in range(2):

        def mix_sent(t, rnd=rnd):
            mix_copy(rnd, 2 * (t // SIDE), lax.rem(t, SIDE)).wait_send()

        over(1, 2 * SIDE, mix_sent)

    def sent(j):
        part_copy(0, j).wait_send()
        part_copy(1, j).wait_send()

    over(0, chunks, sent)


def body(q_in, k_in, v_in, q_gain, k_gain, out_weight, out_bias, out_gate):
    tile = q_in.shape[0]
    depth, width = out_weight.shape
    keys = 2 * CHIPS * tile
    chunks = width // min(OUT_CHUNK, width)
    clips = lax.axis_size("clip")
    vmem = pl.BlockSpec(memory_space=pltpu.VMEM)
    dma = pltpu.SemaphoreType.DMA
    return pl.pallas_call(
        kernel,
        out_shape=pltpu.VMEM((tile, width), jnp.bfloat16),
        in_specs=[vmem] * 5 + [pl.BlockSpec(memory_space=pl.ANY)] + [vmem] * 2,
        out_specs=vmem,
        scratch_shapes=[
            pltpu.VMEM((3, HEADS, tile, HD), jnp.bfloat16),
            pltpu.VMEM((2, 3, keys, HD), jnp.bfloat16),
            pltpu.VMEM((keys, SIDE * tile), jnp.float32),
            pltpu.VMEM((2, 2 * SIDE, tile, HD), jnp.bfloat16),
            pltpu.VMEM((2 * tile, 2 * SIDE * HD), jnp.bfloat16),
            pltpu.VMEM((SIDE, tile, HD), jnp.bfloat16),
            pltpu.VMEM((tile, SIDE * HD), jnp.bfloat16),
            pltpu.VMEM((2, depth, width), jnp.bfloat16),
            pltpu.VMEM((2 * HD, width), jnp.bfloat16),
            pltpu.VMEM((tile, width), jnp.float32),
            pltpu.VMEM((tile, width), jnp.bfloat16),
            pltpu.VMEM((tile, width), jnp.bfloat16),
            dma((3,)),
            dma((CHIPS,)), dma((CHIPS,)),
            dma((CHIPS,)), dma((CHIPS,)),
            dma((SIDE,)), dma((SIDE,)),
            dma((2, SIDE)), dma((2, SIDE)),
            dma((SIDE,)), dma((SIDE,)),
            dma((CHIPS,)), dma((CHIPS,)),
            dma((CHIPS,)), dma((CHIPS,)),
            dma, dma,
            dma((2,)), dma((2,)),
            dma((2, clips)), dma((2, clips)),
            dma((clips,)), dma((clips,)),
            dma((SIDE,)), dma((SIDE,)),
            dma((2, 2 * SIDE)), dma((2, 2 * SIDE)),
            dma((2, chunks)), dma((2, chunks)),
        ],
        compiler_params=pltpu.CompilerParams(
            collective_id=0, has_side_effects=True, vmem_limit_bytes=60 * 1024 * 1024
        ),
        name="attention_branch",
    )(
        q_in, k_in, v_in, q_gain, k_gain, out_weight,
        out_bias.reshape(1, -1), out_gate.reshape(1, -1),
    )


def solution(mesh):
    split = P(("clip", "blk", "head"), None)
    in_specs = (split, split, split, P(), P(), P("head", None), P(), P())
    return jax.shard_map(body, mesh=mesh, in_specs=in_specs, out_specs=split, check_vma=False)
```

time: 73.8 us -> 69.3 us (0.939); the launches traced: 72.7 us -> 69.2 us
  Pallas kernels: 71.6 us -> 68.2 us
    pallas_call x1, Pallas kernels: 71.6 us -> 68.2 us  [body(): pl.pallas_call(kernel, out_shape=pltpu.VMEM((tile, width), jnp.bfloat16),...]
where the time goes in v3:
time: 69.3 us; the launch traced here: 69.2 us
  Pallas kernels  68.2 us (98%)
  local copies, waits for them, and re-layouts  1.06 us (2%)
    pallas_call x1, Pallas kernels, body(): pl.pallas_call(kernel, out_shape=pltpu.VMEM((tile, width), jnp.bfloat16),...  68.2 us

profile of v3, /device:TPU:1, one launch (start us, length us, event | category | flops | bytes accessed | tf_op | source)
XLA Modules:
  0.0 69.2 jit_solution(7342951512529061948)
XLA Ops:
  0.0 68.2 %attention_branch.1 = bf16[128,5120]{1,0:T(8,128)(2,1)S(1)} custom-call(bf16[128,2560]{1,0:T(8,128)(2,1)} %q_ref.1, bf16[128,2560]{1,0:T(8,128)(2,1)} %k_ref.1, bf16[128,2560]{1,0:T(8,128)(2,1)} %v_ref.1, f32[2560]{0:T(1024)} %qg_ref.1, f32[2560]{0:T(1024)} %kg_ref.1, bf16[640,5120]{1,0:T(8,128)(2,1)} %w_ref.1, f32[1,5120]{1,0:T(1,128)} %bitcast.2, ...), custom_call_target="tpu_custom_call" | custom-call | tf_op jit(solution)/shard_map/attention_branch/pallas_call | solution.py:468
  68.2 1.1 %copy.10 = bf16[128,5120]{1,0:T(8,128)(2,1)} copy(bf16[128,5120]{1,0:T(8,128)(2,1)S(1)} %attention_branch.1) | data formatting | bytes 2621440

commit v4 on v3

--- a/solution.py
+++ b/solution.py
@@ -30,7 +30,7 @@
 def kernel(
     q_ref, k_ref, v_ref, qg_ref, kg_ref, w_ref, bias_ref, gate_ref, out_ref,
     stage, qkv, scores, mixed, attended, left_mixed, left_attended, weight, other, own, part_out, part_in,
-    local_sem, full_send, full_recv, late_send, late_recv, left_send, left_recv, row_send, row_recv, relay_send, relay_recv,
+    local_sem, go_sem, full_send, full_recv, late_send, late_recv, left_send, left_recv, row_send, row_recv, relay_send, relay_recv,
     pair_send, pair_recv, pair_left_send, pair_left_recv, w_send, w_recv,
     near_send, near_recv, ring_send, ring_recv, other_send, other_recv, left_mix_send, left_mix_recv,
     mix_send, mix_recv, part_send, part_recv,
@@ -77,20 +77,22 @@
     barrier = pltpu.get_barrier_semaphore()
 
     def greet(r, carry):
-        pl.semaphore_signal(
-            barrier, inc=1, device_id=device(r // SIDE, lax.rem(r, SIDE)), device_id_type=MESH
-        )
+        yy, xx = chip(r // SIDE, lax.rem(r, SIDE))
+        first = {"blk": (yy // 2) * SIDE + xx, "head": lax.rem(yy, 2) * 2}
+        pl.semaphore_signal(barrier, inc=1, device_id=first, device_id_type=MESH)
         return carry
 
     lax.fori_loop(1, CHIPS, greet, 0)
+    beside = [2, clips - 2, 1, clips - 1]
 
     def clip_at(dz):
         return {"clip": lax.rem(z + dz, clips), "blk": blk, "head": head}
 
-    beside = [1, clips - 1] if clips > 2 else [1][: clips - 1]
-    for dz in beside:
-        pl.semaphore_signal(barrier, inc=1, device_id=clip_at(dz), device_id_type=MESH)
-    pl.semaphore_signal(barrier, inc=1, device_id=sibling, device_id_type=MESH)
+    @pl.when(core == 1)
+    def _():
+        pl.semaphore_signal(barrier, inc=1, device_id=sibling, device_id_type=MESH)
+        for dz in beside:
+            pl.semaphore_signal(barrier, inc=1, device_id=clip_at(dz), device_id_type=MESH)
 
     def normalize(ref, gain_ref, which, scale):
         wide = ref[...].astype(jnp.float32)
@@ -107,7 +109,15 @@
     for h in range(HEADS):
         stage[2, h] = v_ref[:, h * HD : (h + 1) * HD].T
 
-    pl.semaphore_wait(barrier, CHIPS + len(beside))
+    @pl.when(core == 0)
+    def _():
+        pl.semaphore_wait(barrier, 2 * CHIPS - 1)
+        pl.semaphore_signal(go_sem, inc=1, device_id=sibling, device_id_type=MESH)
+
+    @pl.when(core == 1)
+    def _():
+        pl.semaphore_wait(go_sem, 1)
+
 
     w_copy = remote(w_ref, weight.at[core], w_send, w_recv, sibling)
     w_copy.start()
@@ -123,35 +133,46 @@
     def slice_of(origin):
         return other.at[pl.ds(pl.multiple_of(origin * 2 * piece, 2 * piece), 2 * piece)]
 
-    def origin_of(d, step):
-        return lax.rem(z + (clips - step if d == 0 else step), clips)
-
-    def ring_copy(d, step):
-        moved = slice_of(origin_of(d, step - 1))
-        return remote(
-            moved, moved, ring_send.at[d, step], ring_recv.at[d, step], clip_at(1 if d == 0 else clips - 1)
-        )
+    def clip_of(dz):
+        return lax.rem(z + dz, clips)
+
+    def ring_copy(k):
+        if k < 4:
+            moved, dz = slice_of(z), beside[k]
+        elif k < 6:
+            moved, dz = slice_of(clip_of(beside[5 - k])), beside[k - 2]
+        else:
+            start = clip_of(beside[7 - k]) * 2 * piece + (k - 6) * piece
+            moved, dz = other.at[pl.ds(pl.multiple_of(start, piece), piece)], beside[k - 6]
+        return remote(moved, moved, ring_send.at[k], ring_recv.at[k], clip_at(dz))
 
     def other_copy(origin):
         return remote(
             slice_of(origin), slice_of(origin), other_send.at[origin], other_recv.at[origin], sibling
         )
-
-    ring_steps = [clips // 2, (clips - 1) // 2]
 
     def ring(step):
         @pl.when(core == 1)
         def _():
             if step == 1:
+                pl.semaphore_wait(barrier, len(beside))
                 near_copy(0).wait_recv()
                 near_copy(1).wait_recv()
+                for k in range(4):
+                    ring_copy(k).start()
                 other_copy(z).start()
-            for d in range(2):
-                if 1 < step <= ring_steps[d] + 1:
-                    ring_copy(d, step - 1).wait_recv()
-                    other_copy(origin_of(d, step - 1)).start()
-                if step <= ring_steps[d]:
-                    ring_copy(d, step).start()
+            elif step == 2:
+                for k in range(4):
+                    ring_copy(k).wait_recv()
+                for k in range(4, 8):
+                    ring_copy(k).start()
+                for dz in beside:
+                    other_copy(clip_of(dz)).start()
+            else:
+                for k in range(4, 8):
+                    ring_copy(k).wait_recv()
+                for dz in (3, 4, 5):
+                    other_copy(clip_of(dz)).start()
 
     def left_copy(dy):
         yy, xx = chip(dy, 0)
@@ -350,7 +371,6 @@
     ring(1)
     over(0, 2, lambda i: attend(0, 2 - 2 * i))
     over(1, SIDE, take_left)
-    ring(2)
     for r in LATE:
         late_copy(r).wait_recv()
     attend(1, 2)
@@ -389,16 +409,15 @@
     w_copy.wait_recv()
     mix_wait(0)
     over(0, chunks, project_sent)
-    ring(3)
     attend(1, 0)
     over(0, SIDE, relay_left)
-    ring(4)
+    ring(2)
     mix_wait(1)
     over(0, chunks, project_kept)
     over(0, SIDE, end_left)
     over(0, CHIPS, lambda i: pair_left_copy(i).wait_recv())
     attend_left()
-    ring(5)
+    ring(3)
     over(1, SIDE, lambda dy: left_mix_copy(dy).wait_recv())
 
     @pl.when(core == 0)
@@ -438,9 +457,8 @@
     def _():
         near_copy(0).wait_send()
         near_copy(1).wait_send()
-        for d in range(2):
-            for step in range(1, ring_steps[d] + 1):
-                ring_copy(d, step).wait_send()
+        for k in range(8):
+            ring_copy(k).wait_send()
         over(0, clips, lambda origin: other_copy(origin).wait_send())
 
     for rnd in range(2):
@@ -484,6 +502,7 @@
             pltpu.VMEM((tile, width), jnp.bfloat16),
             pltpu.VMEM((tile, width), jnp.bfloat16),
             dma((3,)),
+            pltpu.SemaphoreType.REGULAR,
             dma((CHIPS,)), dma((CHIPS,)),
             dma((CHIPS,)), dma((CHIPS,)),
             dma((SIDE,)), dma((SIDE,)),
@@ -493,7 +512,7 @@
             dma((CHIPS,)), dma((CHIPS,)),
             dma, dma,
             dma((2,)), dma((2,)),
-            dma((2, clips)), dma((2, clips)),
+            dma((8,)), dma((8,)),
             dma((clips,)), dma((clips,)),
             dma((SIDE,)), dma((SIDE,)),
             dma((2, 2 * SIDE)), dma((2, 2 * SIDE)),

time: 69.3 us -> 67.3 us (0.971)
  Pallas kernels: 68.2 us -> 66.2 us
    pallas_call x1, Pallas kernels: 68.2 us -> 66.2 us  [body(): pl.pallas_call(kernel, out_shape=pltpu.VMEM((tile, width), jnp.bfloat16),...]
where the time goes in v4:
time: 67.3 us; the launch traced here: 67.2 us
  Pallas kernels  66.2 us (98%)
  local copies, waits for them, and re-layouts  1.06 us (2%)
    pallas_call x1, Pallas kernels, body(): pl.pallas_call(kernel, out_shape=pltpu.VMEM((tile, width), jnp.bfloat16),...  66.2 us

profile of v4, /device:TPU:1, one launch (start us, length us, event | category | flops | bytes accessed | tf_op | source)
XLA Modules:
  0.0 67.2 jit_solution(2764702201126394683)
XLA Ops:
  0.0 66.2 %attention_branch.1 = bf16[128,5120]{1,0:T(8,128)(2,1)S(1)} custom-call(bf16[128,2560]{1,0:T(8,128)(2,1)} %q_ref.1, bf16[128,2560]{1,0:T(8,128)(2,1)} %k_ref.1, bf16[128,2560]{1,0:T(8,128)(2,1)} %v_ref.1, f32[2560]{0:T(1024)} %qg_ref.1, f32[2560]{0:T(1024)} %kg_ref.1, bf16[640,5120]{1,0:T(8,128)(2,1)} %w_ref.1, f32[1,5120]{1,0:T(1,128)} %bitcast.2, ...), custom_call_target="tpu_custom_call" | custom-call | tf_op jit(solution)/shard_map/attention_branch/pallas_call | solution.py:486
  66.2 1.1 %copy.10 = bf16[128,5120]{1,0:T(8,128)(2,1)} copy(bf16[128,5120]{1,0:T(8,128)(2,1)S(1)} %attention_branch.1) | data formatting | bytes 2621440

commit v5 on v4

--- a/solution.py
+++ b/solution.py
@@ -412,11 +412,11 @@
     attend(1, 0)
     over(0, SIDE, relay_left)
     ring(2)
-    mix_wait(1)
-    over(0, chunks, project_kept)
     over(0, SIDE, end_left)
     over(0, CHIPS, lambda i: pair_left_copy(i).wait_recv())
     attend_left()
+    mix_wait(1)
+    over(0, chunks, project_kept)
     ring(3)
     over(1, SIDE, lambda dy: left_mix_copy(dy).wait_recv())
 

time: 67.3 us -> 67 us (level)
  no operation moved by 1% of the time
where the time goes in v5:
time: 67 us; the launch traced here: 66.9 us
  Pallas kernels  65.8 us (98%)
  local copies, waits for them, and re-layouts  1.06 us (2%)
    pallas_call x1, Pallas kernels, body(): pl.pallas_call(kernel, out_shape=pltpu.VMEM((tile, width), jnp.bfloat16),...  65.8 us

profile of v5, /device:TPU:1, one launch (start us, length us, event | category | flops | bytes accessed | tf_op | source)
XLA Modules:
  0.0 66.9 jit_solution(7811063037112803765)
XLA Ops:
  0.0 65.8 %attention_branch.1 = bf16[128,5120]{1,0:T(8,128)(2,1)S(1)} custom-call(bf16[128,2560]{1,0:T(8,128)(2,1)} %q_ref.1, bf16[128,2560]{1,0:T(8,128)(2,1)} %k_ref.1, bf16[128,2560]{1,0:T(8,128)(2,1)} %v_ref.1, f32[2560]{0:T(1024)} %qg_ref.1, f32[2560]{0:T(1024)} %kg_ref.1, bf16[640,5120]{1,0:T(8,128)(2,1)} %w_ref.1, f32[1,5120]{1,0:T(1,128)} %bitcast.2, ...), custom_call_target="tpu_custom_call" | custom-call | tf_op jit(solution)/shard_map/attention_branch/pallas_call | solution.py:486
  65.8 1.1 %copy.10 = bf16[128,5120]{1,0:T(8,128)(2,1)} copy(bf16[128,5120]{1,0:T(8,128)(2,1)S(1)} %attention_branch.1) | data formatting | bytes 2621440
